TPU v7x, 32 devices: a whole 2x2x4 slice. The times are simulated.
32 devices in a mesh: batch: 8 (over y, x, core), patch: 4 (over z).
Axes of the slice: x: 2, y: 2, z: 4, core: 2. Of those that a mesh axis runs over, the one named last changes fastest.
Arguments:
- hidden_in: bfloat16 [12288, 1280], P(('batch', 'patch')), parts along dimension 0, may hold values from -45 to 45
- stale_keys: bfloat16 [12288, 1280], P(('batch', 'patch')), parts along dimension 0, may hold values from -150 to 150
- stale_values: bfloat16 [12288, 1280], P(('batch', 'patch')), parts along dimension 0, may hold values from -12 to 12
- stale_moments: float32 [192, 2, 2, 32], P(('batch', 'patch')), parts along dimension 0, may hold values from -5120 to 102400, as said below
- gain_attn: float32 [1280], replicated, may hold values from 0.1 to 1.9
- bias_attn: float32 [1280], replicated, may hold values from -3 to 3
- w_query: bfloat16 [1280, 1280], replicated, may hold values from -0.3125 to 0.3125
- w_key: bfloat16 [1280, 1280], replicated, may hold values from -0.625 to 0.625
- w_value: bfloat16 [1280, 1280], replicated, may hold values from -0.625 to 0.625
- gain_conv: float32 [1280], replicated, may hold values from 0.1 to 1.9
- bias_conv: float32 [1280], replicated, may hold values from -3 to 3
- conv_weight: bfloat16 [3, 3, 1280, 640], replicated, may hold values from -0.0546875 to 0.0546875
- conv_bias: float32 [640], replicated, may hold values from -3 to 3
- w_time: bfloat16 [320, 640], replicated, may hold values from -0.3125 to 0.3125
- timestep: int32 [1], replicated, may hold values from 0 to 999
Outputs:
- conv_out: bfloat16 [12288, 640], P(('batch', 'patch')), parts along dimension 0
There are 8 independent parts, one for each index of `batch`. A program takes and returns all parts, laid end to end along the dimension named above; an argument that names none is the same for every part. Nothing has to cross between parts.
Inputs may be any that keep to these rules, and one draw needn't show every extreme that they name: `stale_moments`: each row's entries are the sums and sums of squares of 2560 values: that count times the second is at least the square of the first.
All inputs are finite; a program needn't handle non-finite values.
Results may differ from a plain program's by a relative error of at most 0.008.
The roundings to bfloat16 on the way count: a program that leaves them out, or rounds other values in their place, can miss the bound.
Values may be sent and summed in bfloat16 or wider, within the bound.
A program may use at most 320 MiB of HBM per device.

v0:
```python
import math

import jax
import jax.numpy as jnp
from jax import lax
from jax.sharding import PartitionSpec as P

HEADS = 20
GROUPS = 32
W = 64


EPS = 1e-05
NEG = -1e30


def padded_2(cells, sides, width):
    for axis, dim in sides:
        count = lax.axis_size(axis)
        ends = count - 1
        head = lax.slice_in_dim(cells, 0, width, axis=dim)
        tail = lax.slice_in_dim(cells, cells.shape[dim] - width, cells.shape[dim], axis=dim)
        cells = jnp.concatenate(
            [
                lax.ppermute(tail, axis, [(i, (i + 1) % count) for i in range(ends)]),
                cells,
                lax.ppermute(head, axis, [((i + 1) % count, i) for i in range(ends)]),
            ],
            axis=dim,
        )
    return cells


def group_moments(rows_in, groups):
    values = rows_in.astype(jnp.float32).reshape(
        rows_in.shape[0], groups, rows_in.shape[1] // groups
    )
    return jnp.stack([jnp.sum(values, axis=(0, 2)), jnp.sum(values * values, axis=(0, 2))])


def group_normalize(rows_in, totals, count, gain, offset, groups):
    average = totals[0] / count
    variance = totals[1] / count - average * average
    inverse = lax.rsqrt(variance + EPS)
    group_width = rows_in.shape[1] // groups
    factors = jnp.repeat(inverse, group_width) * gain
    shifts = offset - jnp.repeat(average * inverse, group_width) * gain
    return rows_in.astype(jnp.float32) * factors + shifts


def time_embedding(timestep, w_time):
    half_dim = w_time.shape[0] // 2
    frequency = jnp.exp(-math.log(10000.0) * jnp.arange(half_dim, dtype=jnp.float32) / half_dim)
    angles = timestep[0].astype(jnp.float32) * frequency
    embedded = jnp.concatenate([jnp.cos(angles), jnp.sin(angles)])
    return jnp.dot(embedded[None, :], w_time.astype(jnp.float32), precision=lax.Precision.HIGHEST)[
        0
    ]


def body(
    hidden_in,
    stale_keys,
    stale_values,
    stale_moments,
    gain_attn,
    bias_attn,
    w_query,
    w_key,
    w_value,
    gain_conv,
    bias_conv,
    conv_weight,
    conv_bias,
    w_time,
    timestep,
):
    devices = lax.axis_size("patch")
    position = lax.axis_index("patch")
    tok_rows = hidden_in.shape[0]
    channels = hidden_in.shape[1]
    head_dim = channels // HEADS
    all_tokens = tok_rows * devices
    count = all_tokens * (channels // GROUPS)
    scale_qk = head_dim ** (-0.5)
    own_first = position * tok_rows
    own_stale = jnp.sum(stale_moments, axis=0)
    total_attn = lax.psum(own_stale[0], "patch")
    totals_attn = total_attn - own_stale[0] + group_moments(hidden_in, GROUPS)
    normed = group_normalize(hidden_in, totals_attn, count, gain_attn, bias_attn, GROUPS).astype(
        jnp.bfloat16
    )
    query = jnp.dot(normed, w_query, preferred_element_type=jnp.float32).astype(jnp.bfloat16)
    key_fresh = jnp.dot(normed, w_key, preferred_element_type=jnp.float32).astype(jnp.bfloat16)
    value_fresh = jnp.dot(normed, w_value, preferred_element_type=jnp.float32).astype(jnp.bfloat16)
    query3 = query.reshape(tok_rows, HEADS, head_dim)
    key3 = key_fresh.reshape(tok_rows, HEADS, head_dim)
    value3 = value_fresh.reshape(tok_rows, HEADS, head_dim)
    fresh_scores = (
        jnp.einsum("qhd,khd->qhk", query3, key3, preferred_element_type=jnp.float32) * scale_qk
    )
    start_max = jnp.max(fresh_scores, axis=-1)
    fresh_weights = jnp.exp(fresh_scores - start_max[..., None])
    start_sum = jnp.sum(fresh_weights, axis=-1)
    start_acc = jnp.einsum(
        "qhk,khd->qhd",
        fresh_weights.astype(jnp.bfloat16),
        value3,
        preferred_element_type=jnp.float32,
    )
    keys_piece = lax.all_gather(stale_keys, "patch", axis=0, tiled=True)
    values_piece = lax.all_gather(stale_values, "patch", axis=0, tiled=True)
    key_count = keys_piece.shape[0]
    scores = (
        jnp.einsum(
            "qhd,khd->qhk",
            query3,
            keys_piece.reshape(key_count, HEADS, head_dim),
            preferred_element_type=jnp.float32,
        )
        * scale_qk
    )
    key_index = jnp.arange(key_count, dtype=jnp.int32)
    own_keys = (key_index >= own_first) & (key_index < own_first + tok_rows)
    scores = jnp.where(own_keys[None, None, :], NEG, scores)
    max_new = jnp.maximum(start_max, jnp.max(scores, axis=-1))
    rescale_old = jnp.exp(start_max - max_new)
    weights = jnp.exp(scores - max_new[..., None])
    sum_new = start_sum * rescale_old + jnp.sum(weights, axis=-1)
    acc_new = start_acc * rescale_old[..., None] + jnp.einsum(
        "qhk,khd->qhd",
        weights.astype(jnp.bfloat16),
        values_piece.reshape(key_count, HEADS, head_dim),
        preferred_element_type=jnp.float32,
    )
    attended = (acc_new / sum_new[..., None]).reshape(tok_rows, channels)
    updated = (hidden_in.astype(jnp.float32) + attended).astype(jnp.bfloat16)
    total_conv = lax.psum(own_stale[1], "patch")
    totals_conv = total_conv - own_stale[1] + group_moments(updated, GROUPS)
    normed_conv = group_normalize(updated, totals_conv, count, gain_conv, bias_conv, GROUPS)
    activated = jax.nn.silu(normed_conv).astype(jnp.bfloat16).reshape(tok_rows // W, W, channels)
    padded = padded_2(activated, (("patch", 0),), 1)
    convolved = lax.conv_general_dilated(
        padded[None],
        conv_weight,
        (1, 1),
        ((0, 0), (1, 1)),
        dimension_numbers=("NHWC", "HWIO", "NHWC"),
        preferred_element_type=jnp.float32,
    )[0]
    temb = time_embedding(timestep, w_time)
    conv_out = (convolved + conv_bias + temb).astype(jnp.bfloat16)
    return conv_out.reshape(tok_rows, conv_weight.shape[3])


def solution(mesh):
    return jax.shard_map(
        body,
        mesh=mesh,
        in_specs=(
            P(("batch", "patch"), None),
            P(("batch", "patch"), None),
            P(("batch", "patch"), None),
            P(("batch", "patch"), None, None, None),
            P(),
            P(),
            P(),
            P(),
            P(),
            P(),
            P(),
            P(),
            P(),
            P(),
            P(),
        ),
        out_specs=P(("batch", "patch"), None),
        check_vma=False,
    )
```

profile of v0, /device:TPU:0, one launch (start us, length us, event | category | flops | bytes accessed | tf_op | source)
XLA Modules:
  0.0 242.1 jit_solution(17484427149760963255)
XLA Ops:
  6.5 0.7 all-gather.3.cloned.1.call-update
  7.3 0.7 all-gather.5.cloned.1.call-update
  8.0 1.5 convert_reduce_fusion
  9.7 0.1 reduce_sum.97
  9.8 0.1 reduce_sum.76
  9.9 0.7 reduce_sum.73
  10.7 13.6 %all-reduce = (f32[2,32]{1,0:T(2,128)S(1)}, f32[2,32]{1,0:T(2,128)S(1)}) all-reduce(f32[2,32]{1,0:T(2,128)S(1)} %get-tuple-element.25, f32[2,32]{1,0:T(2,128)S(1)} %get-tuple-element.24), channel_id=1, replica_groups=mesh['batch'=8,'patch'=4] {'patch'}, use_global_device_ids=true, to_apply=%region_1.0 | all-reduce | flops 128 | bytes 1024 | tf_op jit(solution)/shard_map/psum | solution.py:88
  24.3 0.1 reshape.91
  24.6 0.7 fusion.64
  25.3 3.6 %convolution_convert_fusion = bf16[384,1280]{1,0:T(8,128)(2,1)} fusion(bf16[1280,1280]{1,0:T(8,128)(2,1)S(1)} %copy-done, bf16[384,1280]{1,0:T(8,128)(2,1)} %param.15, f32[1280]{0:T(1024)S(1)} %get-tuple-element.23, f32[1280]{0:T(1024)S(1)} %get-tuple-element.22), kind=kOutput, calls=%fused_computation.25 | convolution fusion | flops 1260748800 | bytes 5253120 | tf_op jit(solution)/shard_map/dot_general | solution.py:93
  28.9 1.6 copy.52
  30.5 4.8 %convolution_convert_fusion.1 = bf16[384,1280]{1,0:T(8,128)(2,1)} fusion(bf16[1280,1280]{1,0:T(8,128)(2,1)} %param.22, bf16[384,1280]{1,0:T(8,128)(2,1)} %param.15, f32[1280]{0:T(1024)S(1)} %get-tuple-element.23, f32[1280]{0:T(1024)S(1)} %get-tuple-element.22), kind=kOutput, calls=%fused_computation.26 | convolution fusion | flops 1260748800 | bytes 5253120 | tf_op jit(solution)/shard_map/dot_general | solution.py:94
  35.3 1.6 copy.51
  36.9 4.4 %convolution_convert_fusion.2 = bf16[384,1280]{1,0:T(8,128)(2,1)} fusion(bf16[1280,1280]{1,0:T(8,128)(2,1)} %param.23, bf16[384,1280]{1,0:T(8,128)(2,1)S(1)} %copy-done.3, f32[1280]{0:T(1024)S(1)} %get-tuple-element.23, f32[1280]{0:T(1024)S(1)} %get-tuple-element.22), kind=kOutput, calls=%fused_computation.27 | convolution fusion | flops 1260748800 | bytes 5253120 | tf_op jit(solution)/shard_map/dot_general | solution.py:95
  41.2 2.2 copy.50
  44.2 1.7 bitcast_reduce_fusion.1
  45.9 4.2 %copy-done.2 = f32[20,384,384]{2,1,0:T(8,128)} copy-done((f32[20,384,384]{2,1,0:T(8,128)}, f32[20,384,384]{2,1,0:T(8,128)S(1)}, u32[]{:S(2)}) %copy-start.2) | copy-done | bytes 11796504
  50.2 2.0 fusion.7
  52.2 36.0 %all-gather.3.cloned.1.call-done = bf16[1536,1280]{1,0:T(8,128)(2,1)} async-done(((bf16[384,1280]{1,0:T(8,128)(2,1)}), bf16[1536,1280]{1,0:T(8,128)(2,1)}) %all-gather.3.cloned.1.call-update) | async-done | bytes 3932176 | tf_op jit(solution)/shard_map/all_gather | solution.py:111
  88.1 6.3 %copy.54 = bf16[1536,1280]{0,1:T(8,128)(2,1)} copy(bf16[1536,1280]{1,0:T(8,128)(2,1)} %all-gather.3.cloned.1.call-done) | data formatting | bytes 7864320 | tf_op jit(solution)/shard_map/all_gather | solution.py:111
  94.4 20.0 %bitcast_reduce_fusion = (f32[384,20]{0,1:T(8,128)S(1)}, f32[20,384,1536]{2,1,0:T(8,128)}) fusion(pred[1536]{0:T(1024)(128)(4,1)S(1)} %fusion.45, bf16[384,20,64]{0,2,1:T(8,128)(2,1)S(1)} %bitcast.113, bf16[1536,20,64]{0,2,1:T(8,128)(2,1)} %bitcast.111), kind=kOutput, calls=%fused_computation.1 | convolution fusion | flops 1545331200 | bytes 52133376 | tf_op jit(solution)/shard_map/qhd,khd->qhk/dot_general | solution.py:115
  114.4 20.3 %fusion.1 = f32[384,20]{0,1:T(8,128)S(1)} fusion(f32[20,384,1536]{2,1,0:T(8,128)} %get-tuple-element.29, f32[384,20]{0,1:T(8,128)S(1)} %max.13, pred[1536]{0:T(1024)(128)(4,1)S(1)} %fusion.45), kind=kLoop, calls=%fused_computation.4 | loop fusion | flops 47178240 | bytes 47248896 | tf_op jit(solution)/shard_map/reduce_sum | solution.py:129
  134.8 29.9 %all-gather.5.cloned.1.call-done = bf16[1536,1280]{1,0:T(8,128)(2,1)} async-done(((bf16[384,1280]{1,0:T(8,128)(2,1)}), bf16[1536,1280]{1,0:T(8,128)(2,1)}) %all-gather.5.cloned.1.call-update) | async-done | bytes 3932176 | tf_op jit(solution)/shard_map/all_gather | solution.py:112
  164.7 6.3 %copy.55 = bf16[1536,1280]{0,1:T(8,128)(2,1)} copy(bf16[1536,1280]{1,0:T(8,128)(2,1)} %all-gather.5.cloned.1.call-done) | data formatting | bytes 7864320 | tf_op jit(solution)/shard_map/all_gather | solution.py:112
  171.0 21.1 %fusion.3 = f32[20,384,64]{1,2,0:T(8,128)} fusion(bf16[1536,20,64]{0,2,1:T(8,128)(2,1)} %bitcast.117, f32[20,384,1536]{2,1,0:T(8,128)} %get-tuple-element.29, f32[384,20]{0,1:T(8,128)S(1)} %max.13, pred[1536]{0:T(1024)(128)(4,1)S(1)} %fusion.45), kind=kOutput, calls=%fused_computation.6 | convolution fusion | flops 1557135360 | bytes 53116416 | tf_op jit(solution)/shard_map/qhk,khd->qhd/dot_general | solution.py:130
  192.1 8.6 %fusion.26 = f32[384,20,64]{0,2,1:T(8,128)} fusion(f32[20,384,64]{1,2,0:T(8,128)} %fusion.3, bf16[384,20,64]{0,2,1:T(8,128)(2,1)S(1)} %bitcast.120, f32[20,384,384]{2,1,0:T(8,128)} %copy-done.2, f32[384,20]{0,1:T(8,128)S(1)} %get-tuple-element.26, f32[384,20]{0,1:T(8,128)S(1)} %get-tuple-element.14, f32[384,20]{0,1:T(8,128)S(1)} %get-tuple-element.15), kind=kOutput, calls=%fused_computation.41 | convolution fusion | flops 387809280 | bytes 16803840 | tf_op jit(solution)/shard_map/qhk,khd->qhd/dot_general | solution.py:105
  200.7 1.9 copy.56
  202.6 1.3 convert_reduce_fusion.1
  204.0 0.1 reduce_sum.105
  204.2 0.1 reduce_sum.102
  204.4 0.1 reshape.99
  204.7 1.8 fusion.21
  206.5 1.3 collective-permute-start.1
  207.8 4.6 %collective-permute-start = (bf16[1,64,1280]{2,1,0:T(8,128)(2,1)S(1)}, bf16[1,64,1280]{2,1,0:T(8,128)(2,1)S(1)}, u32[]{:S(2)}, u32[]{:S(2)}) collective-permute-start(bf16[1,64,1280]{2,1,0:T(8,128)(2,1)S(1)} %get-tuple-element.18), channel_id=1, source_target_pairs={{0,1},{1,2},{2,3},{4,5},{5,6},{6,7},{8,9},{9,10},{10,11},{12,13},{... | collective-permute-start | bytes 491528 | tf_op jit(solution)/shard_map/ppermute | solution.py:25
  212.5 1.3 convolution_reduce_fusion
  213.8 0.6 copy.58
  214.4 0.3 copy.59
  214.6 0.9 collective-permute-done
  215.6 0.3 copy.57
  215.8 1.1 maximum_bitcast_fusion
  216.9 0.1 pad
  217.0 0.2 copy.61
  217.3 0.2 copy-done.8
  217.6 15.6 %fusion.36 = f32[6,8,9,640]{3,1,2,0:T(8,128)S(1)} fusion(bf16[3,3,1280,640]{3,2,1,0:T(8,128)(2,1)} %param.26, bf16[8,1,7,2,1280]{4,2,3,0,1:T(8,128)(2,1)S(1)} %slice.48, bf16[8,1,8,9,1280]{4,2,3,0,1:T(8,128)(2,1)S(1)} %copy.61, pred[8,9]{0,1:T(8,128)(4,1)S(1)} %copy-done.8), kind=kOutput, calls=%fused_computation.49 | convolution fusion | flops 6375782400 | bytes 17612872 | tf_op jit(solution)/shard_map/conv_general_dilated | solution.py:143
  233.2 0.3 copy.62
  233.6 0.2 copy.63
  233.9 0.9 fusion.40
  234.7 0.6 copy-done.1
  (43 shorter events, 1.4 us)
Async XLA Ops:
  6.5 18.8 %copy-start = (bf16[1280,1280]{1,0:T(8,128)(2,1)S(1)}, bf16[1280,1280]{1,0:T(8,128)(2,1)}, u32[]{:S(2)}) copy-start(bf16[1280,1280]{1,0:T(8,128)(2,1)} %param.21) | copy-start | bytes 9830404
  6.5 81.6 %all-gather.3.cloned.1.call-start = ((), (), s32[]{:S(2)}) async-start(), calls=%async_computation | async-start | bytes 4915200 | tf_op jit(solution)/shard_map/all_gather | solution.py:111
  7.3 157.4 %all-gather.5.cloned.1.call-start = ((), (), s32[]{:S(2)}) async-start(), calls=%async_computation.1 | async-start | bytes 4915200 | tf_op jit(solution)/shard_map/all_gather | solution.py:112
  30.5 6.4 %copy-start.3 = (bf16[384,1280]{1,0:T(8,128)(2,1)S(1)}, bf16[384,1280]{1,0:T(8,128)(2,1)}, u32[]{:S(2)}) copy-start(bf16[384,1280]{1,0:T(8,128)(2,1)} %param.15) | copy-start | bytes 2949124
  45.9 4.2 %copy-start.2 = (f32[20,384,384]{2,1,0:T(8,128)}, f32[20,384,384]{2,1,0:T(8,128)S(1)}, u32[]{:S(2)}) copy-start(f32[20,384,384]{2,1,0:T(8,128)S(1)} %get-tuple-element.27) | copy-start | bytes 35389444
  171.0 21.1 %copy-start.4 = (bf16[384,1280]{0,1:T(8,128)(2,1)S(1)}, bf16[384,1280]{0,1:T(8,128)(2,1)}, u32[]{:S(2)}) copy-start(bf16[384,1280]{0,1:T(8,128)(2,1)} %copy.50) | copy-start | bytes 2949124
  200.7 4.0 %copy-start.5 = (f32[1280]{0:T(1024)S(1)}, f32[1280]{0:T(1024)}, u32[]{:S(2)}) copy-start(f32[1280]{0:T(1024)} %param.24) | copy-start | bytes 15364
  200.7 4.0 %copy-start.6 = (f32[1280]{0:T(1024)S(1)}, f32[1280]{0:T(1024)}, u32[]{:S(2)}) copy-start(f32[1280]{0:T(1024)} %param.25) | copy-start | bytes 15364
  206.5 7.8 %collective-permute-start.1 = (bf16[1,64,1280]{2,1,0:T(8,128)(2,1)S(1)}, bf16[1,64,1280]{2,1,0:T(8,128)(2,1)S(1)}, u32[]{:S(2)}, u32[]{:S(2)}) collective-permute-start(bf16[1,64,1280]{2,1,0:T(8,128)(2,1)S(1)} %get-tuple-element.19), channel_id=1, source_target_pairs={{1,0},{2,1},{3,2},{5,4},{6,5},{7,6},{9,8},{10,9},{11,10},{13,12},{... | collective-permute-start | bytes 491528 | tf_op jit(solution)/shard_map/ppermute | solution.py:27
  207.8 7.7 %collective-permute-start = (bf16[1,64,1280]{2,1,0:T(8,128)(2,1)S(1)}, bf16[1,64,1280]{2,1,0:T(8,128)(2,1)S(1)}, u32[]{:S(2)}, u32[]{:S(2)}) collective-permute-start(bf16[1,64,1280]{2,1,0:T(8,128)(2,1)S(1)} %get-tuple-element.18), channel_id=1, source_target_pairs={{0,1},{1,2},{2,3},{4,5},{5,6},{6,7},{8,9},{9,10},{10,11},{12,13},{... | collective-permute-start | bytes 491528 | tf_op jit(solution)/shard_map/ppermute | solution.py:25
  216.9 0.7 copy-start.8
  233.2 0.7 copy-start.7
  233.2 2.1 copy-start.1
Sparse Core Ops, SparseCore 0:
  8.9 79.1 all-gather.2
  89.7 74.9 all-gather.4
where the time goes:
time: 243 us; the launch traced here: 242 us
  matrix products  81.1 us (33%)
  waiting for transfers between devices  68.2 us (28%)
  other arithmetic  30.9 us (13%)
  local copies, waits for them, and re-layouts  28.1 us (12%)
  between operations  14.4 us (6%)
  blocking collectives  13.6 us (6%)
  starting transfers between devices  5.89 us (2%)
    all_gather x1, waiting for transfers between devices, body(): keys_piece = lax.all_gather(stale_keys, 'patch', axis=0, tiled=True)  36 us
    all_gather x1, waiting for transfers between devices, body(): values_piece = lax.all_gather(stale_values, 'patch', axis=0, tiled=True)  29.9 us
    dot_general x1, matrix products, body(): jnp.einsum('qhk,khd->qhd', weights.astype(jnp.bfloat16), values_piece.res...  21.1 us
    reduce_sum x1, other arithmetic, body(): sum_new = start_sum * rescale_old + jnp.sum(weights, axis=-1)  20.3 us
    dot_general x1, matrix products, body(): jnp.einsum('qhd,khd->qhk', query3, keys_piece.reshape(key_count, HEADS, h...  20 us
    conv_general_dilated x1, matrix products, body(): lax.conv_general_dilated(padded[None], conv_weight, (1, 1), ((0, 0), (1,...  15.6 us
    psum x1, blocking collectives, body(): total_attn = lax.psum(own_stale[0], 'patch')  13.6 us
    dot_general x1, matrix products, body(): jnp.einsum('qhk,khd->qhd', fresh_weights.astype(jnp.bfloat16), value3, pr...  8.59 us
  transfers between devices with their start and end apart: 4, of which 3 were waited for; matrix products, arithmetic and copies ran while one was open for 31% of the time, Pallas kernels for 0%

commit v1 on v0

v1 whole, which is shorter than its diff:
```python
import functools
import math

import jax
import jax.numpy as jnp
from jax import lax
from jax.experimental import pallas as pl
from jax.experimental.pallas import tpu as pltpu
from jax.sharding import PartitionSpec as P

HEADS = 20
GROUPS = 32
W = 64
EPS = 1e-05
PW = 128
AHEAD = 2
F32 = jnp.float32
BF16 = jnp.bfloat16
HI = lax.Precision.HIGHEST


def is_lent(n, p):
    if n < 4:
        return p < 0
    return (lax.rem(p, 2) == 0) & (p >= 2)


def lent_index(p):
    return jnp.maximum(lax.div(p, 2) - 1, 0)


def kernel(
    n,
    hidden_hbm,
    keys_hbm,
    values_hbm,
    moments_ref,
    gain_a,
    bias_a,
    gain_c,
    bias_c,
    wqkv_q,
    wqkv_k,
    wqkv_v,
    wconv_hbm,
    bias_out,
    out_ref,
    hid,
    wq,
    wconv,
    kv,
    q_ref,
    q_in,
    lent_out,
    lent_in,
    stat_out,
    stat_in,
    sbuf,
    ot,
    upd,
    act,
    ybuf,
    sums,
    rows_n,
    mom,
    local_sem,
    send_r,
    send_l,
    recv,
    mom_send,
    mom_recv,
    lend_send,
    lend_recv,
    halo_send,
    halo_recv,
):
    me = lax.axis_index("patch")
    tok, chan = hid.shape
    pairs = chan // PW
    count = n * tok * (chan // GROUPS)
    last = n - 1
    has_left, has_right = me > 0, me < last
    is_end = (me == 0) | (me == last)
    is_server = ((me == 1) | (me == n - 2)) if n >= 4 else (me < 0)
    served = jnp.where(me == 1, 0, last)
    server = jnp.where(me == 0, 1, last - 1)

    def remote(src, dst, ssem, rsem, to):
        return pltpu.make_async_remote_copy(
            src_ref=src,
            dst_ref=dst,
            send_sem=ssem,
            recv_sem=rsem,
            device_id={"patch": to},
            device_id_type=pl.DeviceIdType.MESH,
        )

    barrier = pltpu.get_barrier_semaphore()

    @pl.when(has_left)
    def _():
        pl.semaphore_signal(
            barrier, inc=1, device_id={"patch": me - 1}, device_id_type=pl.DeviceIdType.MESH
        )

    @pl.when(has_right)
    def _():
        pl.semaphore_signal(
            barrier, inc=1, device_id={"patch": me + 1}, device_id_type=pl.DeviceIdType.MESH
        )

    load_hid = pltpu.make_async_copy(hidden_hbm, hid, local_sem.at[0])
    load_hid.start()
    load_w = [
        pltpu.make_async_copy(w, wq.at[i], local_sem.at[1 + i])
        for i, w in enumerate((wqkv_q, wqkv_k, wqkv_v))
    ]
    for c in load_w:
        c.start()

    own_row = jnp.sum(moments_ref[...], axis=0, keepdims=True)
    mom[me] = jnp.broadcast_to(own_row, (8, 128))

    pl.semaphore_wait(barrier, has_left.astype(jnp.int32) + has_right.astype(jnp.int32))

    def mom_copy(s, right):
        return remote(
            mom.at[s],
            mom.at[s],
            mom_send.at[s, 1 if right else 0],
            mom_recv.at[s],
            me + 1 if right else me - 1,
        )

    @pl.when(has_right)
    def _():
        mom_copy(me, True).start()

    @pl.when(has_left)
    def _():
        mom_copy(me, False).start()

    def goes(right, p):
        if right:
            return has_right & jnp.logical_not(is_lent(n, p) & (me + 1 == last))
        return has_left & jnp.logical_not(is_lent(n, p) & (me - 1 == 0))

    def kv_copy(p, s, c, right, src=None):
        dst = kv.at[c, p, s]
        return remote(
            dst if src is None else src,
            dst,
            (send_r if right else send_l).at[p, s, c],
            recv.at[p, s, c],
            me + 1 if right else me - 1,
        )

    def send_own(p):
        cols = pl.ds(pl.multiple_of(p * PW, PW), PW)
        for right in (True, False):

            @pl.when(goes(right, p))
            def _():
                for c, ref in enumerate((keys_hbm, values_hbm)):
                    kv_copy(p, me, c, right, ref.at[:, cols]).start()

    for p in range(AHEAD):
        send_own(jnp.int32(p))

    load_conv = pltpu.make_async_copy(wconv_hbm, wconv, local_sem.at[4])
    load_conv.start()

    def own_copies(p):
        cols = pl.ds(pl.multiple_of(p * PW, PW), PW)
        return [
            pltpu.make_async_copy(ref.at[:, cols], kv.at[c, p, n], local_sem.at[5 + c])
            for c, ref in enumerate((keys_hbm, values_hbm))
        ]

    load_hid.wait()

    def column_sums(i, carry):
        a, b = carry
        x = hid[pl.ds(pl.multiple_of(i * W, W), W), :].astype(F32)
        return (
            a + jnp.sum(x, axis=0, keepdims=True),
            b + jnp.sum(x * x, axis=0, keepdims=True),
        )

    zero_row = jnp.zeros((1, chan), F32)
    sum_x, sum_xx = lax.fori_loop(0, tok // W, column_sums, (zero_row, zero_row))

    for j in range(1, n):

        @pl.when(me - j >= 0)
        def _():
            mom_copy(me - j, True).wait_recv()

            @pl.when(has_right)
            def _():
                mom_copy(me - j, True).start()

        @pl.when(me + j <= last)
        def _():
            mom_copy(me + j, False).wait_recv()

            @pl.when(has_left)
            def _():
                mom_copy(me + j, False).start()

    def others(s, row):
        return row + jnp.where(s == me, 0.0, mom[s])

    other_rows = lax.fori_loop(0, n, others, jnp.zeros((8, 128), F32))
    mom_total = jnp.broadcast_to(other_rows[0:1], (8, 128))

    group_of = lax.div(lax.broadcasted_iota(jnp.int32, (chan, 128), 0), chan // GROUPS)
    lane_of = lax.broadcasted_iota(jnp.int32, (chan, 128), 1)

    def spread(k):
        return (lane_of == group_of + k * GROUPS).astype(F32)

    def factors(norm, s_x, s_xx, gain, offset):
        e_sum, e_sq = spread(2 * norm), spread(2 * norm + 1)
        own = jnp.dot(
            jnp.broadcast_to(s_x, (8, chan)), e_sum, precision=HI, preferred_element_type=F32
        ) + jnp.dot(
            jnp.broadcast_to(s_xx, (8, chan)), e_sq, precision=HI, preferred_element_type=F32
        )
        totals = mom_total + own
        nt = (((1,), (1,)), ((), ()))
        first = lax.dot_general(totals, e_sum, nt, precision=HI, preferred_element_type=F32)
        second = lax.dot_general(totals, e_sq, nt, precision=HI, preferred_element_type=F32)
        average = first[0:1] / count
        variance = second[0:1] / count - average * average
        inverse = lax.rsqrt(variance + EPS)
        rows_n[0:1, :] = inverse * gain
        rows_n[1:2, :] = offset - average * inverse * gain

    factors(0, sum_x, sum_xx, gain_a[...], bias_a[...])

    def normalize(i, _):
        rows = pl.ds(pl.multiple_of(i * W, W), W)
        upd[rows, :] = (hid[rows, :].astype(F32) * rows_n[0:1, :] + rows_n[1:2, :]).astype(BF16)
        return 0

    lax.fori_loop(0, tok // W, normalize, 0)
    for c in load_w:
        c.wait()
    scale = (chan // HEADS) ** (-0.5)

    def project(j, _):
        cols = pl.ds(pl.multiple_of(j * 2 * PW, 2 * PW), 2 * PW)
        for i in range(3):
            r = jnp.dot(upd[...], wq[i, :, cols], preferred_element_type=F32).astype(BF16)
            for half in range(2):
                piece = r[:, half * PW : (half + 1) * PW]
                if i == 0:
                    q_ref[2 * j + half] = (piece.astype(F32) * scale).astype(BF16)
                else:
                    kv[i - 1, 2 * j + half, me] = piece
        return 0

    lax.fori_loop(0, chan // (2 * PW), project, 0)

    def q_copy(f):
        return remote(
            q_ref.at[2 * f + 2], q_in.at[f], lend_send.at[0, f], lend_recv.at[0, f], server
        )

    def lent_copy(f):
        return remote(
            lent_out.at[f], lent_in.at[f], lend_send.at[1, f], lend_recv.at[1, f], served
        )

    def stat_copy(f):
        return remote(
            stat_out.at[f], stat_in.at[f], lend_send.at[2, f], lend_recv.at[2, f], served
        )

    n_lent = q_in.shape[0]
    if n >= 4:

        @pl.when(is_end)
        def _():
            for f in range(n_lent):
                q_copy(f).start()

    lane = lax.broadcasted_iota(jnp.int32, (tok, PW), 1)

    def attend(q, p, shards, slot_of):
        q32 = q.astype(F32)
        halves = [
            jnp.where((lane >= h * 64) & (lane < h * 64 + 64), q32, 0.0).astype(BF16)
            for h in range(2)
        ]

        def score(j, tops):
            k = kv[0, p, slot_of(j)]
            new = []
            for h in range(2):
                sc = lax.dot_general(
                    k, halves[h], (((1,), (1,)), ((), ())), preferred_element_type=F32
                )
                sbuf[h, j] = sc
                new.append(jnp.maximum(tops[h], jnp.max(sc, axis=0, keepdims=True)))
            return tuple(new)

        low = jnp.full((1, tok), -jnp.inf, F32)
        tops = lax.fori_loop(0, shards, score, (low, low))

        def weigh(j, carry):
            v = kv[1, p, slot_of(j)]
            new = []
            for h in range(2):
                total, acc = carry[h]
                wts = jnp.exp(sbuf[h, j] - tops[h])
                part = lax.dot_general(
                    v[:, h * 64 : h * 64 + 64],
                    wts.astype(BF16),
                    (((0,), (0,)), ((), ())),
                    preferred_element_type=F32,
                )
                new.append((total + jnp.sum(wts, axis=0, keepdims=True), acc + part))
            return tuple(new)

        zero = (jnp.zeros((1, tok), F32), jnp.zeros((64, tok), F32))
        sums_h = lax.fori_loop(0, shards, weigh, (zero, zero))
        return [(tops[h], sums_h[h][0], sums_h[h][1]) for h in range(2)]

    def step(p, _):
        cols = pl.ds(pl.multiple_of(p * PW, PW), PW)
        lent = is_lent(n, p)
        f = lent_index(p)

        @pl.when(p + AHEAD < pairs)
        def _():
            send_own(p + AHEAD)

        serve = lent & is_server
        alone = lent & is_end

        @pl.when(serve)
        def _():
            for c in own_copies(p):
                c.start()

        @pl.when(jnp.logical_not(alone))
        def _():
            for j in range(1, n):

                @pl.when(me - j >= 0)
                def _():
                    for c in range(2):
                        kv_copy(p, me - j, c, True).wait_recv()

                        @pl.when(goes(True, p))
                        def _():
                            kv_copy(p, me - j, c, True).start()

                @pl.when(me + j <= last)
                def _():
                    for c in range(2):
                        kv_copy(p, me + j, c, False).wait_recv()

                        @pl.when(goes(False, p))
                        def _():
                            kv_copy(p, me + j, c, False).start()

        if n >= 4:

            @pl.when(serve)
            def _():
                for c in own_copies(p):
                    c.wait()
                q_copy(f).wait_recv()

                def slot(j):
                    s = j + jnp.where(served == 0, 1, 0)
                    return jnp.where(s == me, n, s)

                for h, (top, total, acc) in enumerate(attend(q_in[f], p, n - 1, slot)):
                    lent_out[f, h * 64 : h * 64 + 64, :] = (acc / total).astype(BF16)
                    stat_out[f, h : h + 1, :] = top
                    stat_out[f, 2 + h : 3 + h, :] = total
                stat_out[f, 4:8, :] = jnp.zeros((4, tok), F32)
                lent_copy(f).start()
                stat_copy(f).start()

        shards = jnp.where(alone, 1, n)
        mine = attend(q_ref[p], p, shards, lambda j: jnp.where(alone, me, j))

        @pl.when(jnp.logical_not(alone))
        def _():
            for h, (top, total, acc) in enumerate(mine):
                ot[h * 64 : h * 64 + 64, :] = acc / total

        if n >= 4:

            @pl.when(alone)
            def _():
                lent_copy(f).wait_recv()
                stat_copy(f).wait_recv()
                for h, (top, total, acc) in enumerate(mine):
                    top_b = stat_in[f, h : h + 1, :]
                    total_b = stat_in[f, 2 + h : 3 + h, :]
                    high = jnp.maximum(top, top_b)
                    fac_a = jnp.exp(top - high)
                    fac_b = jnp.exp(top_b - high) * total_b
                    got = lent_in[f, h * 64 : h * 64 + 64, :].astype(F32)
                    ot[h * 64 : h * 64 + 64, :] = (acc * fac_a + got * fac_b) / (
                        total * fac_a + fac_b
                    )

        new = (hid[:, cols].astype(F32) + ot[...].T).astype(BF16)
        upd[:, cols] = new
        new32 = new.astype(F32)
        sums[0:1, cols] = jnp.sum(new32, axis=0, keepdims=True)
        sums[1:2, cols] = jnp.sum(new32 * new32, axis=0, keepdims=True)
        return 0

    lax.fori_loop(0, pairs, step, 0)

    factors(1, sums[0:1, :], sums[1:2, :], gain_c[...], bias_c[...])
    image_rows = tok // W

    def activate(i):
        x = upd[pl.ds(pl.multiple_of(i * W, W), W), :].astype(F32)
        v = x * rows_n[0:1, :] + rows_n[1:2, :]
        act[pl.ds(pl.multiple_of(i * W + W, W), W), :] = (v / (1.0 + jnp.exp(-v))).astype(BF16)

    activate(jnp.int32(0))
    activate(jnp.int32(image_rows - 1))
    up = remote(
        act.at[pl.ds(W, W)],
        act.at[pl.ds(tok + W, W)],
        halo_send.at[0],
        halo_recv.at[0],
        me - 1,
    )
    down = remote(
        act.at[pl.ds(tok, W)], act.at[pl.ds(0, W)], halo_send.at[1], halo_recv.at[1], me + 1
    )

    @pl.when(has_left)
    def _():
        up.start()

    @pl.when(has_right)
    def _():
        down.start()

    lax.fori_loop(1, image_rows - 1, lambda i, c: (activate(i), c)[1], 0)
    load_conv.wait()

    def middle_tap(b, _):
        ybuf[b] = jnp.dot(act[W : W + tok, :], wconv[3 + b], preferred_element_type=F32)
        return 0

    lax.fori_loop(0, 3, middle_tap, 0)

    @pl.when(has_right)
    def _():
        up.wait_recv()

    @pl.when(jnp.logical_not(has_right))
    def _():
        act[tok + W : tok + 2 * W, :] = jnp.zeros((W, chan), BF16)

    @pl.when(has_left)
    def _():
        down.wait_recv()

    @pl.when(jnp.logical_not(has_left))
    def _():
        act[0:W, :] = jnp.zeros((W, chan), BF16)

    def outer_tap(t, _):
        a, b = lax.div(t, 3) * 2, lax.rem(t, 3)
        rows = pl.ds(pl.multiple_of(a * W, W), tok)
        ybuf[b] += jnp.dot(act[rows, :], wconv[a * 3 + b], preferred_element_type=F32)
        return 0

    lax.fori_loop(0, 6, outer_tap, 0)

    cout = out_ref.shape[1]
    column = lax.rem(lax.broadcasted_iota(jnp.int32, (tok, cout), 0), W)
    before = jnp.where(column == 0, 0.0, pltpu.roll(ybuf[0], 1, 0))
    after = jnp.where(column == W - 1, 0.0, pltpu.roll(ybuf[2], tok - 1, 0))
    out_ref[...] = (before + ybuf[1] + after + bias_out[...]).astype(BF16)

    def drain(p, _):
        for right in (True, False):
            for j in range(n):
                s = me - j if right else me + j
                ok = (s >= 0) if right else (s <= last)

                @pl.when(goes(right, p) & ok)
                def _():
                    for c in range(2):
                        kv_copy(p, s, c, right).wait_send()

        return 0

    lax.fori_loop(0, pairs, drain, 0)
    for j in range(n):

        @pl.when(has_right & (me - j >= 0))
        def _():
            mom_copy(me - j, True).wait_send()

        @pl.when(has_left & (me + j <= last))
        def _():
            mom_copy(me + j, False).wait_send()

    if n >= 4:

        @pl.when(is_end)
        def _():
            for f in range(n_lent):
                q_copy(f).wait_send()

        @pl.when(is_server)
        def _():
            for f in range(n_lent):
                lent_copy(f).wait_send()
                stat_copy(f).wait_send()

    @pl.when(has_left)
    def _():
        up.wait_send()

    @pl.when(has_right)
    def _():
        down.wait_send()


def time_embedding(timestep, w_time):
    half_dim = w_time.shape[0] // 2
    frequency = jnp.exp(-math.log(10000.0) * jnp.arange(half_dim, dtype=jnp.float32) / half_dim)
    angles = timestep[0].astype(jnp.float32) * frequency
    embedded = jnp.concatenate([jnp.cos(angles), jnp.sin(angles)])
    return jnp.dot(embedded[None, :], w_time.astype(jnp.float32), precision=lax.Precision.HIGHEST)


def body(
    n,
    hidden_in,
    stale_keys,
    stale_values,
    stale_moments,
    gain_attn,
    bias_attn,
    w_query,
    w_key,
    w_value,
    gain_conv,
    bias_conv,
    conv_weight,
    conv_bias,
    w_time,
    timestep,
):
    tok, chan = hidden_in.shape
    cout = conv_weight.shape[3]
    pairs = chan // PW
    lent = 4
    bias_out = time_embedding(timestep, w_time) + conv_bias[None, :]
    vmem = pl.BlockSpec(memory_space=pltpu.VMEM)
    hbm = pl.BlockSpec(memory_space=pl.ANY)
    dma = pltpu.SemaphoreType.DMA
    return pl.pallas_call(
        functools.partial(kernel, n),
        out_shape=jax.ShapeDtypeStruct((tok, cout), BF16),
        in_specs=[hbm] * 3 + [vmem] * 5 + [hbm] * 4 + [vmem],
        out_specs=vmem,
        scratch_shapes=[
            pltpu.VMEM((tok, chan), BF16),
            pltpu.VMEM((3, chan, chan), BF16),
            pltpu.VMEM((9, chan, cout), BF16),
            pltpu.VMEM((2, pairs, n + 1, tok, PW), BF16),
            pltpu.VMEM((pairs, tok, PW), BF16),
            pltpu.VMEM((lent, tok, PW), BF16),
            pltpu.VMEM((lent, PW, tok), BF16),
            pltpu.VMEM((lent, PW, tok), BF16),
            pltpu.VMEM((lent, 8, tok), F32),
            pltpu.VMEM((lent, 8, tok), F32),
            pltpu.VMEM((2, n, tok, tok), F32),
            pltpu.VMEM((PW, tok), F32),
            pltpu.VMEM((tok, chan), BF16),
            pltpu.VMEM((tok + 2 * W, chan), BF16),
            pltpu.VMEM((3, tok, cout), F32),
            pltpu.VMEM((8, chan), F32),
            pltpu.VMEM((8, chan), F32),
            pltpu.VMEM((n, 8, 128), F32),
            dma((8,)),
            dma((pairs, n, 2)),
            dma((pairs, n, 2)),
            dma((pairs, n, 2)),
            dma((n, 2)),
            dma((n,)),
            dma((3, lent)),
            dma((3, lent)),
            dma((2,)),
            dma((2,)),
        ],
        compiler_params=pltpu.CompilerParams(
            collective_id=0,
            has_side_effects=True,
            vmem_limit_bytes=63 * 1024 * 1024,
        ),
        cost_estimate=pl.CostEstimate(
            flops=2 * tok * chan * (3 * chan + 2 * n * tok + 9 * cout),
            bytes_accessed=2 * (3 * chan * chan + 9 * chan * cout + 4 * tok * chan),
            transcendentals=HEADS * n * tok * tok,
        ),
    )(
        hidden_in,
        stale_keys,
        stale_values,
        stale_moments.reshape(stale_moments.shape[0], 128),
        gain_attn[None, :],
        bias_attn[None, :],
        gain_conv[None, :],
        bias_conv[None, :],
        w_query,
        w_key,
        w_value,
        conv_weight.reshape(9, chan, cout),
        bias_out,
    )


def solution(mesh):
    split = P(("batch", "patch"), None)
    return jax.shard_map(
        functools.partial(body, mesh.shape["patch"]),
        mesh=mesh,
        in_specs=(split, split, split, P(("batch", "patch"), None, None, None)) + (P(),) * 11,
        out_specs=split,
        check_vma=False,
    )
```

time: 243 us -> 168 us (0.69)
  Pallas kernels: 0 us -> 156 us
  matrix products: 81.1 us -> 0.29 us
  waiting for transfers between devices: 68.2 us -> 0 us
  other arithmetic: 30.9 us -> 0.82 us
  local copies, waits for them, and re-layouts: 28.1 us -> 9.17 us
  between operations: 14.4 us -> 0.73 us
  blocking collectives: 13.6 us -> 0 us
  starting transfers between devices: 5.89 us -> 0 us
    pallas_call x0 -> x1, Pallas kernels: none -> 156 us  [body(): pl.pallas_call(functools.partial(kernel, n), out_shape=jax.ShapeDtypeStru...]
    all_gather x2 -> x0, waiting for transfers between devices: 65.9 us -> none  [the longest x1 36 us: body(): keys_piece = lax.all_gather(stale_keys, 'patch', axis=0, tiled=True)]
    dot_general x7 -> x0, matrix products: 64.2 us -> none  [the longest x1 21.1 us: body(): jnp.einsum('qhk,khd->qhd', weights.astype(jnp.bfloat16), values_piece.res...]
    reduce_sum x9 -> x0, other arithmetic: 26.3 us -> none  [the longest x1 20.3 us: body(): sum_new = start_sum * rescale_old + jnp.sum(weights, axis=-1)]
    conv_general_dilated x1 -> x0, matrix products: 15.6 us -> none  [body(): lax.conv_general_dilated(padded[None], conv_weight, (1, 1), ((0, 0), (1,...]
    psum x1 -> x0, blocking collectives: 13.6 us -> none  [body(): total_attn = lax.psum(own_stale[0], 'patch')]
    all_gather x2 -> x0, local copies, waits for them, and re-layouts: 12.6 us -> none  [the longest x1 6.32 us: body(): keys_piece = lax.all_gather(stale_keys, 'patch', axis=0, tiled=True)]
    ppermute x2 -> x0, starting transfers between devices: 5.85 us -> none  [the longest x1 4.56 us: padded_2(): lax.ppermute(tail, axis, [(i, (i + 1) % count) for i in range(ends)])]
  transfers between devices with their start and end apart: 4 -> 0, of which waited for: 3 -> 0; matrix products, arithmetic and copies ran while one was open for 31% -> 0% of each run, Pallas kernels for 0% -> 0%
where the time goes in v1:
time: 168 us; the launch traced here: 167 us
  Pallas kernels  156 us (93%)
  local copies, waits for them, and re-layouts  9.17 us (5%)
    pallas_call x1, Pallas kernels, body(): pl.pallas_call(functools.partial(kernel, n), out_shape=jax.ShapeDtypeStru...  156 us

profile of v1, /device:TPU:0, one launch (start us, length us, event | category | flops | bytes accessed | tf_op | source)
XLA Modules:
  0.0 167.1 jit_solution(17732112687587094046)
XLA Ops:
  0.0 0.0 copy-start
  0.8 0.1 pad_maximum_fusion
  0.8 0.2 copy-done
  1.0 0.3 convolution_reduce_fusion
  1.3 0.7 add.5
  2.0 0.6 add.6.bias_out
  2.6 1.4 reshape.11.moments_ref
  4.0 1.3 broadcast_in_dim.14.gain_a
  5.3 1.3 broadcast_in_dim.15.bias_a
  6.6 1.3 broadcast_in_dim.16.gain_c
  7.8 1.3 broadcast_in_dim.17.bias_c
  9.1 156.1 %shard_map.145 = bf16[384,640]{1,0:T(8,128)(2,1)} custom-call(bf16[384,1280]{1,0:T(8,128)(2,1)} %hidden_hbm.1, bf16[384,1280]{1,0:T(8,128)(2,1)} %keys_hbm.1, bf16[384,1280]{1,0:T(8,128)(2,1)} %values_hbm.1, f32[6,128]{1,0:T(8,128)} %reshape.11.moments_ref, f32[1,1280]{1,0:T(1,128)} %broadcast_in_dim.14.gain_a, f32[1,1280]{1,0:T(1,128)} %broadcast_in_dim.15.bias_a, ...), custom_call_target="tpu_custom_call" | custom-call | flops 12457082880 | bytes 28508160 | tf_op jit(solution)/shard_map/pallas_call | solution.py:572
  165.3 1.9 %copy.18 = bf16[384,640]{1,0:T(8,128)(2,1)} copy(bf16[384,640]{1,0:T(8,128)(2,1)} %shard_map.145) | data formatting | bytes 983040
  (2 shorter events, 0.1 us)
Async XLA Ops:
  0.0 1.0 copy-start

commit v2 on v1

--- a/solution.py
+++ b/solution.py
@@ -13,7 +13,6 @@
 W = 64
 EPS = 1e-05
 PW = 128
-AHEAD = 2
 F32 = jnp.float32
 BF16 = jnp.bfloat16
 HI = lax.Precision.HIGHEST
@@ -164,8 +163,38 @@
                 for c, ref in enumerate((keys_hbm, values_hbm)):
                     kv_copy(p, me, c, right, ref.at[:, cols]).start()
 
-    for p in range(AHEAD):
-        send_own(jnp.int32(p))
+    def forward(p, j):
+        @pl.when(has_right & (me - j >= 0))
+        def _():
+            for c in range(2):
+                kv_copy(p, me - j, c, True).wait_recv()
+
+                @pl.when(goes(True, p))
+                def _():
+                    kv_copy(p, me - j, c, True).start()
+
+        @pl.when(has_left & (me + j <= last))
+        def _():
+            for c in range(2):
+                kv_copy(p, me + j, c, False).wait_recv()
+
+                @pl.when(goes(False, p))
+                def _():
+                    kv_copy(p, me + j, c, False).start()
+
+    def pump(t):
+        @pl.when(t < pairs)
+        def _():
+            send_own(t)
+
+        for j in range(1, n - 1):
+
+            @pl.when((t - j >= 0) & (t - j < pairs))
+            def _():
+                forward(t - j, j)
+
+    send_own(jnp.int32(0))
+    send_own(jnp.int32(1))
 
     load_conv = pltpu.make_async_copy(wconv_hbm, wconv, local_sem.at[4])
     load_conv.start()
@@ -247,9 +276,17 @@
     lax.fori_loop(0, tok // W, normalize, 0)
     for c in load_w:
         c.wait()
+    for j in range(1, n - 1):
+        if j < 2:
+            forward(jnp.int32(0), j)
     scale = (chan // HEADS) ** (-0.5)
 
     def project(j, _):
+        @pl.when(j == 2)
+        def _():
+            for t in range(2, n - 1):
+                pump(jnp.int32(t))
+
         cols = pl.ds(pl.multiple_of(j * 2 * PW, 2 * PW), 2 * PW)
         for i in range(3):
             r = jnp.dot(upd[...], wq[i, :, cols], preferred_element_type=F32).astype(BF16)
@@ -333,9 +370,7 @@
         lent = is_lent(n, p)
         f = lent_index(p)
 
-        @pl.when(p + AHEAD < pairs)
-        def _():
-            send_own(p + AHEAD)
+        pump(p + n - 1)
 
         serve = lent & is_server
         alone = lent & is_end
@@ -345,27 +380,17 @@
             for c in own_copies(p):
                 c.start()
 
-        @pl.when(jnp.logical_not(alone))
-        def _():
-            for j in range(1, n):
-
-                @pl.when(me - j >= 0)
-                def _():
-                    for c in range(2):
-                        kv_copy(p, me - j, c, True).wait_recv()
-
-                        @pl.when(goes(True, p))
-                        def _():
-                            kv_copy(p, me - j, c, True).start()
-
-                @pl.when(me + j <= last)
-                def _():
-                    for c in range(2):
-                        kv_copy(p, me + j, c, False).wait_recv()
-
-                        @pl.when(goes(False, p))
-                        def _():
-                            kv_copy(p, me + j, c, False).start()
+        for j in range(1, n):
+
+            @pl.when(jnp.logical_not(alone | has_right) & (me - j >= 0))
+            def _():
+                for c in range(2):
+                    kv_copy(p, me - j, c, True).wait_recv()
+
+            @pl.when(jnp.logical_not(alone | has_left) & (me + j <= last))
+            def _():
+                for c in range(2):
+                    kv_copy(p, me + j, c, False).wait_recv()
 
         if n >= 4:
 

time: 168 us -> 131 us (0.78)
  Pallas kernels: 156 us -> 120 us
    pallas_call x1, Pallas kernels: 156 us -> 120 us  [body(): pl.pallas_call(functools.partial(kernel, n), out_shape=jax.ShapeDtypeStru...]
where the time goes in v2:
time: 131 us
  Pallas kernels  120 us (92%)
  local copies, waits for them, and re-layouts  9.17 us (7%)
    pallas_call x1, Pallas kernels, body(): pl.pallas_call(functools.partial(kernel, n), out_shape=jax.ShapeDtypeStru...  120 us

profile of v2, /device:TPU:0, one launch (start us, length us, event | category | flops | bytes accessed | tf_op | source)
XLA Modules:
  0.0 130.8 jit_solution(15560997245860218411)
XLA Ops:
  0.0 0.0 copy-start
  0.8 0.1 pad_maximum_fusion
  0.8 0.2 copy-done
  1.0 0.3 convolution_reduce_fusion
  1.3 0.7 add.5
  2.0 0.6 add.6.bias_out
  2.6 1.4 %reshape.11.moments_ref = f32[6,128]{1,0:T(8,128)} reshape(f32[6,2,2,32]{3,2,1,0:T(2,128)} %param.18) | data formatting | bytes 6144 | tf_op jit(solution)/shard_map/reshape | solution.py:646
  4.0 1.3 broadcast_in_dim.14.gain_a
  5.3 1.3 broadcast_in_dim.15.bias_a
  6.6 1.3 broadcast_in_dim.16.gain_c
  7.8 1.3 broadcast_in_dim.17.bias_c
  9.1 119.8 %shard_map.145 = bf16[384,640]{1,0:T(8,128)(2,1)} custom-call(bf16[384,1280]{1,0:T(8,128)(2,1)} %hidden_hbm.1, bf16[384,1280]{1,0:T(8,128)(2,1)} %keys_hbm.1, bf16[384,1280]{1,0:T(8,128)(2,1)} %values_hbm.1, f32[6,128]{1,0:T(8,128)} %reshape.11.moments_ref, f32[1,1280]{1,0:T(1,128)} %broadcast_in_dim.14.gain_a, f32[1,1280]{1,0:T(1,128)} %broadcast_in_dim.15.bias_a, ...), custom_call_target="tpu_custom_call" | custom-call | flops 12457082880 | bytes 28508160 | tf_op jit(solution)/shard_map/pallas_call | solution.py:597
  128.9 1.9 %copy.18 = bf16[384,640]{1,0:T(8,128)(2,1)} copy(bf16[384,640]{1,0:T(8,128)(2,1)} %shard_map.145) | data formatting | bytes 983040
  (2 shorter events, 0.1 us)
Async XLA Ops:
  0.0 1.0 copy-start

commit v3 on v2

--- a/solution.py
+++ b/solution.py
@@ -33,16 +33,12 @@
     hidden_hbm,
     keys_hbm,
     values_hbm,
-    moments_ref,
-    gain_a,
-    bias_a,
-    gain_c,
-    bias_c,
+    moments_hbm,
+    params,
     wqkv_q,
     wqkv_k,
     wqkv_v,
     wconv_hbm,
-    bias_out,
     out_ref,
     hid,
     wq,
@@ -62,6 +58,7 @@
     sums,
     rows_n,
     mom,
+    mom_own,
     local_sem,
     send_r,
     send_l,
@@ -110,6 +107,8 @@
 
     load_hid = pltpu.make_async_copy(hidden_hbm, hid, local_sem.at[0])
     load_hid.start()
+    load_mom = pltpu.make_async_copy(moments_hbm, mom_own, local_sem.at[7])
+    load_mom.start()
     load_w = [
         pltpu.make_async_copy(w, wq.at[i], local_sem.at[1 + i])
         for i, w in enumerate((wqkv_q, wqkv_k, wqkv_v))
@@ -117,7 +116,11 @@
     for c in load_w:
         c.start()
 
-    own_row = jnp.sum(moments_ref[...], axis=0, keepdims=True)
+    load_mom.wait()
+    own4 = jnp.sum(mom_own[...], axis=0)
+    own_row = jnp.concatenate(
+        [own4[i, k : k + 1, :] for i in range(2) for k in range(2)], axis=1
+    )
     mom[me] = jnp.broadcast_to(own_row, (8, 128))
 
     pl.semaphore_wait(barrier, has_left.astype(jnp.int32) + has_right.astype(jnp.int32))
@@ -266,7 +269,7 @@
         rows_n[0:1, :] = inverse * gain
         rows_n[1:2, :] = offset - average * inverse * gain
 
-    factors(0, sum_x, sum_xx, gain_a[...], bias_a[...])
+    factors(0, sum_x, sum_xx, params[0:1, :], params[1:2, :])
 
     def normalize(i, _):
         rows = pl.ds(pl.multiple_of(i * W, W), W)
@@ -325,45 +328,35 @@
 
     lane = lax.broadcasted_iota(jnp.int32, (tok, PW), 1)
 
-    def attend(q, p, shards, slot_of):
+    def attend(q, p, slots):
         q32 = q.astype(F32)
-        halves = [
-            jnp.where((lane >= h * 64) & (lane < h * 64 + 64), q32, 0.0).astype(BF16)
-            for h in range(2)
-        ]
-
-        def score(j, tops):
-            k = kv[0, p, slot_of(j)]
-            new = []
+        both = jnp.concatenate(
+            [
+                jnp.where((lane >= h * 64) & (lane < h * 64 + 64), q32, 0.0).astype(BF16)
+                for h in range(2)
+            ],
+            axis=0,
+        )
+        top = jnp.full((1, 2 * tok), -jnp.inf, F32)
+        for j, slot in enumerate(slots):
+            sc = lax.dot_general(
+                kv[0, p, slot], both, (((1,), (1,)), ((), ())), preferred_element_type=F32
+            )
+            sbuf[j] = sc
+            top = jnp.maximum(top, jnp.max(sc, axis=0, keepdims=True))
+
+        totals = [jnp.zeros((1, tok), F32)] * 2
+        accs = [jnp.zeros((64, tok), F32)] * 2
+        for j, slot in enumerate(slots):
+            v = kv[1, p, slot].T
             for h in range(2):
-                sc = lax.dot_general(
-                    k, halves[h], (((1,), (1,)), ((), ())), preferred_element_type=F32
+                cols = slice(h * tok, h * tok + tok)
+                wts = jnp.exp(sbuf[j, :, cols] - top[:, cols])
+                totals[h] += jnp.sum(wts, axis=0, keepdims=True)
+                accs[h] += jnp.dot(
+                    v[h * 64 : h * 64 + 64, :], wts.astype(BF16), preferred_element_type=F32
                 )
-                sbuf[h, j] = sc
-                new.append(jnp.maximum(tops[h], jnp.max(sc, axis=0, keepdims=True)))
-            return tuple(new)
-
-        low = jnp.full((1, tok), -jnp.inf, F32)
-        tops = lax.fori_loop(0, shards, score, (low, low))
-
-        def weigh(j, carry):
-            v = kv[1, p, slot_of(j)]
-            new = []
-            for h in range(2):
-                total, acc = carry[h]
-                wts = jnp.exp(sbuf[h, j] - tops[h])
-                part = lax.dot_general(
-                    v[:, h * 64 : h * 64 + 64],
-                    wts.astype(BF16),
-                    (((0,), (0,)), ((), ())),
-                    preferred_element_type=F32,
-                )
-                new.append((total + jnp.sum(wts, axis=0, keepdims=True), acc + part))
-            return tuple(new)
-
-        zero = (jnp.zeros((1, tok), F32), jnp.zeros((64, tok), F32))
-        sums_h = lax.fori_loop(0, shards, weigh, (zero, zero))
-        return [(tops[h], sums_h[h][0], sums_h[h][1]) for h in range(2)]
+        return [(top[:, h * tok : h * tok + tok], totals[h], accs[h]) for h in range(2)]
 
     def step(p, _):
         cols = pl.ds(pl.multiple_of(p * PW, PW), PW)
@@ -404,7 +397,9 @@
                     s = j + jnp.where(served == 0, 1, 0)
                     return jnp.where(s == me, n, s)
 
-                for h, (top, total, acc) in enumerate(attend(q_in[f], p, n - 1, slot)):
+                for h, (top, total, acc) in enumerate(
+                    attend(q_in[f], p, [slot(j) for j in range(n - 1)])
+                ):
                     lent_out[f, h * 64 : h * 64 + 64, :] = (acc / total).astype(BF16)
                     stat_out[f, h : h + 1, :] = top
                     stat_out[f, 2 + h : 3 + h, :] = total
@@ -412,18 +407,16 @@
                 lent_copy(f).start()
                 stat_copy(f).start()
 
-        shards = jnp.where(alone, 1, n)
-        mine = attend(q_ref[p], p, shards, lambda j: jnp.where(alone, me, j))
-
         @pl.when(jnp.logical_not(alone))
         def _():
-            for h, (top, total, acc) in enumerate(mine):
+            for h, (top, total, acc) in enumerate(attend(q_ref[p], p, range(n))):
                 ot[h * 64 : h * 64 + 64, :] = acc / total
 
         if n >= 4:
 
             @pl.when(alone)
             def _():
+                mine = attend(q_ref[p], p, [me])
                 lent_copy(f).wait_recv()
                 stat_copy(f).wait_recv()
                 for h, (top, total, acc) in enumerate(mine):
@@ -446,7 +439,7 @@
 
     lax.fori_loop(0, pairs, step, 0)
 
-    factors(1, sums[0:1, :], sums[1:2, :], gain_c[...], bias_c[...])
+    factors(1, sums[0:1, :], sums[1:2, :], params[2:3, :], params[3:4, :])
     image_rows = tok // W
 
     def activate(i):
@@ -512,7 +505,7 @@
     column = lax.rem(lax.broadcasted_iota(jnp.int32, (tok, cout), 0), W)
     before = jnp.where(column == 0, 0.0, pltpu.roll(ybuf[0], 1, 0))
     after = jnp.where(column == W - 1, 0.0, pltpu.roll(ybuf[2], tok - 1, 0))
-    out_ref[...] = (before + ybuf[1] + after + bias_out[...]).astype(BF16)
+    out_ref[...] = (before + ybuf[1] + after + params[4:5, 0:cout]).astype(BF16)
 
     def drain(p, _):
         for right in (True, False):
@@ -591,13 +584,15 @@
     pairs = chan // PW
     lent = 4
     bias_out = time_embedding(timestep, w_time) + conv_bias[None, :]
+    rows = [gain_attn, bias_attn, gain_conv, bias_conv, jnp.pad(bias_out[0], (0, chan - cout))]
+    params = jnp.stack(rows + [jnp.zeros((chan,), F32)] * 3)
     vmem = pl.BlockSpec(memory_space=pltpu.VMEM)
     hbm = pl.BlockSpec(memory_space=pl.ANY)
     dma = pltpu.SemaphoreType.DMA
     return pl.pallas_call(
         functools.partial(kernel, n),
         out_shape=jax.ShapeDtypeStruct((tok, cout), BF16),
-        in_specs=[hbm] * 3 + [vmem] * 5 + [hbm] * 4 + [vmem],
+        in_specs=[hbm] * 4 + [vmem] + [hbm] * 4,
         out_specs=vmem,
         scratch_shapes=[
             pltpu.VMEM((tok, chan), BF16),
@@ -610,7 +605,7 @@
             pltpu.VMEM((lent, PW, tok), BF16),
             pltpu.VMEM((lent, 8, tok), F32),
             pltpu.VMEM((lent, 8, tok), F32),
-            pltpu.VMEM((2, n, tok, tok), F32),
+            pltpu.VMEM((n, tok, 2 * tok), F32),
             pltpu.VMEM((PW, tok), F32),
             pltpu.VMEM((tok, chan), BF16),
             pltpu.VMEM((tok + 2 * W, chan), BF16),
@@ -618,6 +613,7 @@
             pltpu.VMEM((8, chan), F32),
             pltpu.VMEM((8, chan), F32),
             pltpu.VMEM((n, 8, 128), F32),
+            pltpu.VMEM(stale_moments.shape, F32),
             dma((8,)),
             dma((pairs, n, 2)),
             dma((pairs, n, 2)),
@@ -643,16 +639,12 @@
         hidden_in,
         stale_keys,
         stale_values,
-        stale_moments.reshape(stale_moments.shape[0], 128),
-        gain_attn[None, :],
-        bias_attn[None, :],
-        gain_conv[None, :],
-        bias_conv[None, :],
+        stale_moments,
+        params,
         w_query,
         w_key,
         w_value,
         conv_weight.reshape(9, chan, cout),
-        bias_out,
     )
 
 

time: 131 us -> 125 us (0.954)
  local copies, waits for them, and re-layouts: 9.17 us -> 5.53 us
  Pallas kernels: 120 us -> 117 us
    broadcast_in_dim x4 -> x0, local copies, waits for them, and re-layouts: 5.16 us -> none  [the longest x1 1.29 us: body(): gain_attn[None, :]]
    another operation x0 -> x8, local copies, waits for them, and re-layouts: none -> 3.49 us  [body(): params = jnp.stack(rows + [jnp.zeros((chan,), F32)] * 3)]
    pallas_call x1, Pallas kernels: 120 us -> 117 us  [body(): pl.pallas_call(functools.partial(kernel, n), out_shape=jax.ShapeDtypeStru...]
    reshape x1 -> x0, local copies, waits for them, and re-layouts: 1.37 us -> none  [body(): stale_moments.reshape(stale_moments.shape[0], 128)]
where the time goes in v3:
time: 125 us
  Pallas kernels  117 us (94%)
  local copies, waits for them, and re-layouts  5.53 us (4%)
    pallas_call x1, Pallas kernels, body(): pl.pallas_call(functools.partial(kernel, n), out_shape=jax.ShapeDtypeStru...  117 us
    another operation x8, local copies, waits for them, and re-layouts, body(): params = jnp.stack(rows + [jnp.zeros((chan,), F32)] * 3)  3.49 us

profile of v3, /device:TPU:0, one launch (start us, length us, event | category | flops | bytes accessed | tf_op | source)
XLA Modules:
  0.0 124.6 jit_solution(14335770881546452843)
XLA Ops:
  0.0 0.0 copy-start
  0.8 0.1 pad_maximum_fusion
  0.8 0.2 copy-done
  1.0 0.3 convolution_reduce_fusion
  1.3 0.7 add.6
  2.0 0.7 stack.21
  2.7 0.7 stack.22
  3.4 0.7 stack.23
  4.1 0.7 stack.24
  4.8 0.7 stack.27.params
  5.5 117.2 %shard_map.145 = bf16[384,640]{1,0:T(8,128)(2,1)} custom-call(bf16[384,1280]{1,0:T(8,128)(2,1)} %hidden_hbm.1, bf16[384,1280]{1,0:T(8,128)(2,1)} %keys_hbm.1, bf16[384,1280]{1,0:T(8,128)(2,1)} %values_hbm.1, f32[6,2,2,32]{3,2,1,0:T(2,128)} %moments_hbm.1, f32[8,1280]{1,0:T(8,128)} %stack.27.params, bf16[1280,1280]{1,0:T(8,128)(2,1)} %wqkv_q.1, ...), custom_call_target="tpu_custom_call" | custom-call | flops 12457082880 | bytes 28508160 | tf_op jit(solution)/shard_map/pallas_call | solution.py:592
  122.7 1.9 %copy.18 = bf16[384,640]{1,0:T(8,128)(2,1)} copy(bf16[384,640]{1,0:T(8,128)(2,1)} %shard_map.145) | data formatting | bytes 983040
  (6 shorter events, 0.1 us)
Async XLA Ops:
  0.0 1.0 copy-start

commit v4 on v3

--- a/solution.py
+++ b/solution.py
@@ -186,9 +186,9 @@
                     kv_copy(p, me + j, c, False).start()
 
     def pump(t):
-        @pl.when(t < pairs)
-        def _():
-            send_own(t)
+        @pl.when(t + 1 < pairs)
+        def _():
+            send_own(t + 1)
 
         for j in range(1, n - 1):
 
@@ -198,6 +198,7 @@
 
     send_own(jnp.int32(0))
     send_own(jnp.int32(1))
+    send_own(jnp.int32(2))
 
     load_conv = pltpu.make_async_copy(wconv_hbm, wconv, local_sem.at[4])
     load_conv.start()

time: 125 us -> 128 us (1.024)
  Pallas kernels: 117 us -> 120 us
    pallas_call x1, Pallas kernels: 117 us -> 120 us  [body(): pl.pallas_call(functools.partial(kernel, n), out_shape=jax.ShapeDtypeStru...]
where the time goes in v4:
time: 128 us
  Pallas kernels  120 us (94%)
  local copies, waits for them, and re-layouts  5.53 us (4%)
    pallas_call x1, Pallas kernels, body(): pl.pallas_call(functools.partial(kernel, n), out_shape=jax.ShapeDtypeStru...  120 us
    another operation x8, local copies, waits for them, and re-layouts, body(): params = jnp.stack(rows + [jnp.zeros((chan,), F32)] * 3)  3.49 us

profile of v4, /device:TPU:0, one launch (start us, length us, event | category | flops | bytes accessed | tf_op | source)
XLA Modules:
  0.0 127.7 jit_solution(16568030611716043368)
XLA Ops:
  0.0 0.0 copy-start
  0.8 0.1 pad_maximum_fusion
  0.8 0.2 copy-done
  1.0 0.3 convolution_reduce_fusion
  1.3 0.7 add.6
  2.0 0.7 stack.21
  2.7 0.7 stack.22
  3.4 0.7 stack.23
  4.1 0.7 stack.24
  4.8 0.7 stack.27.params
  5.5 120.3 %shard_map.145 = bf16[384,640]{1,0:T(8,128)(2,1)} custom-call(bf16[384,1280]{1,0:T(8,128)(2,1)} %hidden_hbm.1, bf16[384,1280]{1,0:T(8,128)(2,1)} %keys_hbm.1, bf16[384,1280]{1,0:T(8,128)(2,1)} %values_hbm.1, f32[6,2,2,32]{3,2,1,0:T(2,128)} %moments_hbm.1, f32[8,1280]{1,0:T(8,128)} %stack.27.params, bf16[1280,1280]{1,0:T(8,128)(2,1)} %wqkv_q.1, ...), custom_call_target="tpu_custom_call" | custom-call | flops 12457082880 | bytes 28508160 | tf_op jit(solution)/shard_map/pallas_call | solution.py:593
  125.9 1.9 %copy.18 = bf16[384,640]{1,0:T(8,128)(2,1)} copy(bf16[384,640]{1,0:T(8,128)(2,1)} %shard_map.145) | data formatting | bytes 983040
  (6 shorter events, 0.1 us)
Async XLA Ops:
  0.0 1.0 copy-start
